TPU v7x, 32 devices: a whole 2x2x4 slice. The times are simulated.
32 devices in a mesh: grp: 2 (over x), seq: 16 (over z, y, core).
Axes of the slice: x: 2, y: 2, z: 4, core: 2. Of those that a mesh axis runs over, the one named last changes fastest.
Arguments:
- raw_queries: bfloat16 [4096, 4096], P(('grp', 'seq')), parts along dimension 0, as said below
- beacon_queries: bfloat16 [128, 4096], P(('grp', 'seq')), parts along dimension 0, may hold values from -6 to 6
- raw_keys: bfloat16 [4096, 512], P(('grp', 'seq')), parts along dimension 0, as said below
- raw_values: bfloat16 [4096, 512], P(('grp', 'seq')), parts along dimension 0, may hold values from -6 to 6
- beacon_keys: bfloat16 [128, 512], P(('grp', 'seq')), parts along dimension 0, may hold values from -6 to 6
- beacon_values: bfloat16 [128, 512], P(('grp', 'seq')), parts along dimension 0, may hold values from -6 to 6
- raw_cotangent: bfloat16 [4096, 4096], P(('grp', 'seq')), parts along dimension 0, may hold values from -6 to 6
- beacon_cotangent: bfloat16 [128, 4096], P(('grp', 'seq')), parts along dimension 0, may hold values from -6 to 6
- slot_span: int32 [32], P('grp'), parts along dimension 0, may hold values from 0 to 15, each once
- beacon_counts: int32 [32], P('grp'), parts along dimension 0, may hold values from 1 to 4, as said below
- first_span: int32 [32], P('grp'), parts along dimension 0, may hold values from 0 to 15, as said below
Outputs:
- raw_query_grad: bfloat16 [4096, 4096], P(('grp', 'seq')), parts along dimension 0
- beacon_query_grad: bfloat16 [128, 4096], P(('grp', 'seq')), parts along dimension 0
- raw_key_grad: bfloat16 [4096, 512], P(('grp', 'seq')), parts along dimension 0
- raw_value_grad: bfloat16 [4096, 512], P(('grp', 'seq')), parts along dimension 0
- beacon_key_grad: bfloat16 [128, 512], P(('grp', 'seq')), parts along dimension 0
- beacon_value_grad: bfloat16 [128, 512], P(('grp', 'seq')), parts along dimension 0
There are 2 independent parts, one for each index of `grp`. A program takes and returns all parts, laid end to end along the dimension named above; each array names one. Nothing has to cross between parts.
Inputs may be any that keep to these rules, and one draw needn't show every extreme that they name: `raw_queries`: queries and keys lie within -6 to 6. `raw_keys`: keys lie within -6 to 6. `beacon_counts`: some span has exactly 4 live beacons and some span exactly one. first_span[c] <= c, it never falls along c, first_span[0] is 0, where first_span[c] differs from first_span[c-1] it equals c, and the last span begins a document of its own.
All inputs are finite; a program needn't handle non-finite values.
Results may differ from a plain program's by a relative error of at most 0.0065.
Values may be sent and summed in bfloat16 or wider, within the bound.
A program may use at most 64 MiB of HBM per device.

v0:
```python
import jax
import jax.numpy as jnp
from jax import lax
from jax.sharding import PartitionSpec as P

HEADS = 32
KV_HEADS = 4
HEAD_DIM = 128
SPAN = 128
BEACONS = 4


def lookup(lookup_table, positions):
    width_count = lookup_table.shape[0]
    hits = positions[:, None] == jnp.arange(width_count)[None, :]
    return jnp.sum(jnp.where(hits, lookup_table[None, :], 0), axis=1)


def select_entry(entries, slot_index):
    return jnp.sum(jnp.where(jnp.arange(entries.shape[0]) == slot_index, entries, 0))


def visible(slot_span, beacon_counts, first_span, slot_index):
    span_count = slot_span.shape[0]
    slot_counts = lookup(beacon_counts, slot_span)
    slot_first = lookup(first_span, slot_span)
    own_span = select_entry(slot_span, slot_index)
    own_first = select_entry(slot_first, slot_index)
    own_count = select_entry(slot_counts, slot_index)
    key_span = jnp.repeat(slot_span, BEACONS)
    key_slot = jnp.repeat(jnp.arange(span_count), BEACONS)
    key_beacon = jnp.tile(jnp.arange(BEACONS), span_count)
    key_live = key_beacon < jnp.repeat(slot_counts, BEACONS)
    earlier = (own_first <= key_span) & (key_span < own_span) & key_live
    raw_ids = jnp.arange(SPAN)
    beacon_ids = jnp.arange(BEACONS)
    raw_part = jnp.concatenate(
        [
            jnp.broadcast_to(earlier[None, :], (SPAN, earlier.shape[0])),
            raw_ids[None, :] <= raw_ids[:, None],
        ],
        axis=1,
    )
    own_beacons = (
        (key_slot[None, :] == slot_index)
        & (key_beacon[None, :] <= beacon_ids[:, None])
        & key_live[None, :]
    )
    beacon_part = jnp.concatenate(
        [earlier[None, :] | own_beacons, jnp.ones((BEACONS, SPAN), bool)], axis=1
    )
    allowed = jnp.concatenate([raw_part, beacon_part], axis=0)
    live_rows = jnp.concatenate([jnp.ones((SPAN,), bool), beacon_ids < own_count])
    return (allowed, live_rows)


def head_slices(queries, cotangents, kv_head):
    group_size = HEADS // KV_HEADS
    row_count = queries.shape[0]
    low = kv_head * group_size * HEAD_DIM
    high = (kv_head + 1) * group_size * HEAD_DIM
    q_head = queries[:, low:high].reshape(row_count, group_size, HEAD_DIM)
    g_head = cotangents[:, low:high].reshape(row_count, group_size, HEAD_DIM)
    return (q_head, g_head)


def slot_pass(queries, cotangents, key_rows, value_rows, allowed):
    score_scale = HEAD_DIM ** (-0.5)
    row_count = queries.shape[0]
    group_size = HEADS // KV_HEADS
    query_parts, key_parts, value_parts, statistics = ([], [], [], [])
    for kv_head in range(KV_HEADS):
        q_head, g_head = head_slices(queries, cotangents, kv_head)
        k_head = key_rows[:, kv_head * HEAD_DIM : (kv_head + 1) * HEAD_DIM]
        v_head = value_rows[:, kv_head * HEAD_DIM : (kv_head + 1) * HEAD_DIM]
        scores = (
            jnp.einsum("mgd,nd->gmn", q_head, k_head, preferred_element_type=jnp.float32)
            * score_scale
        )
        scores = jnp.where(allowed[None], scores, -1e30)
        row_max = jnp.max(scores, axis=-1, keepdims=True)
        row_total = jnp.sum(jnp.exp(scores - row_max), axis=-1, keepdims=True)
        logsum = row_max + jnp.log(row_total)
        attention = jnp.exp(scores - logsum)
        attention_grad = jnp.einsum(
            "mgd,nd->gmn", g_head, v_head, preferred_element_type=jnp.float32
        )
        row_delta = jnp.sum(attention * attention_grad, axis=-1, keepdims=True)
        score_grad = (attention * (attention_grad - row_delta) * score_scale).astype(jnp.bfloat16)
        attention_low = attention.astype(jnp.bfloat16)
        query_parts.append(
            jnp.einsum(
                "gmn,nd->mgd", score_grad, k_head, preferred_element_type=jnp.float32
            ).reshape(row_count, group_size * HEAD_DIM)
        )
        key_parts.append(
            jnp.einsum("gmn,mgd->nd", score_grad, q_head, preferred_element_type=jnp.float32)
        )
        value_parts.append(
            jnp.einsum("gmn,mgd->nd", attention_low, g_head, preferred_element_type=jnp.float32)
        )
        statistics.append((logsum, row_delta))
    return (
        jnp.concatenate(query_parts, axis=1).astype(jnp.bfloat16),
        jnp.concatenate(key_parts, axis=1),
        jnp.concatenate(value_parts, axis=1),
        statistics,
    )


def local(
    raw_queries,
    beacon_queries,
    raw_keys,
    raw_values,
    beacon_keys,
    beacon_values,
    raw_cotangent,
    beacon_cotangent,
    slot_span,
    beacon_counts,
    first_span,
):
    slots_here = beacon_keys.shape[0] // BEACONS
    kv_width = KV_HEADS * HEAD_DIM
    all_keys, all_values = (
        lax.all_gather(beacon_keys, "seq", axis=0, tiled=True),
        lax.all_gather(beacon_values, "seq", axis=0, tiled=True),
    )
    beacon_total = all_keys.shape[0]
    first_slot = lax.axis_index("seq") * slots_here
    raw_query_parts, beacon_query_parts, raw_key_parts, raw_value_parts, kept_slots = (
        [],
        [],
        [],
        [],
        [],
    )
    slot_index = first_slot + 0
    queries = jnp.concatenate([raw_queries, beacon_queries], axis=0)
    cotangents = jnp.concatenate([raw_cotangent, beacon_cotangent], axis=0)
    allowed, live_rows = visible(slot_span, beacon_counts, first_span, slot_index)
    cotangents = jnp.where(live_rows[:, None], cotangents, jnp.zeros_like(cotangents))
    key_rows = jnp.concatenate([all_keys, raw_keys], axis=0)
    value_rows = jnp.concatenate([all_values, raw_values], axis=0)
    query_grad, key_grad, value_grad, statistics = slot_pass(
        queries, cotangents, key_rows, value_rows, allowed
    )
    beacon_term = jnp.concatenate([key_grad[:beacon_total], value_grad[:beacon_total]], axis=1)
    raw_key_parts.append(key_grad[beacon_total:].astype(jnp.bfloat16))
    raw_value_parts.append(value_grad[beacon_total:].astype(jnp.bfloat16))
    raw_query_parts.append(query_grad[:SPAN])
    beacon_query_parts.append(query_grad[SPAN:])
    summed = lax.psum_scatter(beacon_term, "seq", scatter_dimension=0, tiled=True)
    raw_query_grad = raw_query_parts[0]
    beacon_query_grad = beacon_query_parts[0]
    raw_key_grad = raw_key_parts[0]
    raw_value_grad = raw_value_parts[0]
    beacon_key_grad = summed[:, :kv_width].astype(jnp.bfloat16)
    beacon_value_grad = summed[:, kv_width:].astype(jnp.bfloat16)
    return (
        raw_query_grad,
        beacon_query_grad,
        raw_key_grad,
        raw_value_grad,
        beacon_key_grad,
        beacon_value_grad,
    )


def solution(mesh):
    in_specs = (
        P(("grp", "seq"), None),
        P(("grp", "seq"), None),
        P(("grp", "seq"), None),
        P(("grp", "seq"), None),
        P(("grp", "seq"), None),
        P(("grp", "seq"), None),
        P(("grp", "seq"), None),
        P(("grp", "seq"), None),
        P("grp"),
        P("grp"),
        P("grp"),
    )
    out_specs = (
        P(("grp", "seq"), None),
        P(("grp", "seq"), None),
        P(("grp", "seq"), None),
        P(("grp", "seq"), None),
        P(("grp", "seq"), None),
        P(("grp", "seq"), None),
    )
    return jax.shard_map(local, mesh=mesh, in_specs=in_specs, out_specs=out_specs, check_vma=False)
```

profile of v0, /device:TPU:0, one launch (start us, length us, event | category | flops | bytes accessed | tf_op | source)
XLA Modules:
  0.0 204.3 jit_solution(3405359780296764700)
XLA Ops:
  0.7 1.4 select_reduce_fusion.3
  2.0 1.2 dynamic-slice
  3.9 0.9 select_reduce_fusion.1
  6.1 2.0 compare_and_fusion
  8.8 23.5 %all-gather = bf16[16,4,512]{2,1,0:T(4,128)(2,1)S(1)} all-gather(bf16[1,4,512]{2,1,0:T(4,128)(2,1)} %bitcast.147), channel_id=1, replica_groups=mesh['grp'=2,'seq'=16] {'seq'}, dimensions={0}, use_global_device_ids=true | all-gather | bytes 69632 | tf_op jit(solution)/shard_map/all_gather | solution.py:127
  32.3 17.9 %all-gather.1 = bf16[16,4,512]{2,1,0:T(4,128)(2,1)S(1)} all-gather(bf16[1,4,512]{2,1,0:T(4,128)(2,1)} %bitcast.148), channel_id=1, replica_groups=mesh['grp'=2,'seq'=16] {'seq'}, dimensions={0}, use_global_device_ids=true | all-gather | bytes 69632 | tf_op jit(solution)/shard_map/all_gather | solution.py:128
  50.3 0.9 constant_dynamic-update-slice_fusion.4
  51.2 0.9 constant_dynamic-update-slice_fusion
  52.9 1.3 convolution_bitcast_fusion.3
  54.2 1.3 convolution_bitcast_fusion.2
  55.5 1.3 convolution_bitcast_fusion.1
  56.8 1.3 convolution_bitcast_fusion
  59.2 0.7 slice.126
  59.9 0.7 slice.124
  62.5 8.5 %convolution_bitcast_fusion.11 = f32[192,128]{1,0:T(8,128)} fusion(f32[8,132,192]{2,1,0:T(8,128)} %convolution_bitcast_fusion.3, f32[8,132,192]{2,1,0:T(8,128)S(1)} %get-tuple-element.21, f32[8,132]{1,0:T(8,128)S(1)} %log_add_fusion.3, bf16[132,8,128]{2,1,0:T(8,128)(2,1)S(1)} %slice.122), kind=kOutput, calls=%fused_computation.51 | convolution fusion | flops 53325024 | bytes 1994880 | tf_op jit(solution)/shard_map/gmn,mgd->nd/dot_general | solution.py:97
  71.0 7.5 %fusion.28 = bf16[132,8,128]{2,0,1:T(8,128)(2,1)S(1)} fusion(f32[8,132,192]{2,1,0:T(8,128)} %convolution_bitcast_fusion.3, f32[8,132,192]{2,1,0:T(8,128)S(1)} %get-tuple-element.21, f32[8,132]{1,0:T(8,128)S(1)} %log_add_fusion.3, bf16[192,512]{1,0:T(8,128)(2,1)S(1)} %constant_dynamic-update-slice_fusion), kind=kOutput, calls=%fused_computation.40 | convolution fusion | flops 53460192 | bytes 4792320 | tf_op jit(solution)/shard_map/gmn,nd->mgd/dot_general | solution.py:92
  78.6 0.8 copy-done.1
  79.4 1.4 fusion.131
  82.0 8.5 %convolution_bitcast_fusion.10 = f32[192,128]{1,0:T(8,128)} fusion(f32[8,132,192]{2,1,0:T(8,128)} %convolution_bitcast_fusion.2, f32[8,132,192]{2,1,0:T(8,128)S(1)} %get-tuple-element.23, f32[8,132]{1,0:T(8,128)S(1)} %log_add_fusion.2, bf16[132,8,128]{2,1,0:T(8,128)(2,1)} %slice.124), kind=kOutput, calls=%fused_computation.50 | convolution fusion | flops 53325024 | bytes 1994880 | tf_op jit(solution)/shard_map/gmn,mgd->nd/dot_general | solution.py:97
  90.5 8.2 %fusion.29 = bf16[132,8,128]{2,0,1:T(8,128)(2,1)} fusion(f32[8,132,192]{2,1,0:T(8,128)} %convolution_bitcast_fusion.2, f32[8,132,192]{2,1,0:T(8,128)S(1)} %get-tuple-element.23, f32[8,132]{1,0:T(8,128)S(1)} %log_add_fusion.2, bf16[192,512]{1,0:T(8,128)(2,1)} %copy-done.8), kind=kOutput, calls=%fused_computation.41 | convolution fusion | flops 53460192 | bytes 4792320 | tf_op jit(solution)/shard_map/gmn,nd->mgd/dot_general | solution.py:92
  98.8 1.0 copy.62
  100.0 1.4 fusion.132
  101.9 1.3 convolution_bitcast_fusion.5
  103.2 8.6 %convolution_bitcast_fusion.9 = f32[192,128]{1,0:T(8,128)} fusion(f32[8,132,192]{2,1,0:T(8,128)} %convolution_bitcast_fusion.1, f32[8,132,192]{2,1,0:T(8,128)S(1)} %get-tuple-element.25, f32[8,132]{1,0:T(8,128)S(1)} %log_add_fusion.1, bf16[132,8,128]{2,1,0:T(8,128)(2,1)S(1)} %copy-done), kind=kOutput, calls=%fused_computation.49 | convolution fusion | flops 53325024 | bytes 1994880 | tf_op jit(solution)/shard_map/gmn,mgd->nd/dot_general | solution.py:97
  111.7 8.1 %fusion.30 = bf16[132,8,128]{2,0,1:T(8,128)(2,1)} fusion(f32[8,132,192]{2,1,0:T(8,128)} %convolution_bitcast_fusion.1, f32[8,132,192]{2,1,0:T(8,128)S(1)} %get-tuple-element.25, f32[8,132]{1,0:T(8,128)S(1)} %log_add_fusion.1, bf16[192,512]{1,0:T(8,128)(2,1)} %copy-done.8), kind=kOutput, calls=%fused_computation.42 | convolution fusion | flops 53460192 | bytes 4792320 | tf_op jit(solution)/shard_map/gmn,nd->mgd/dot_general | solution.py:92
  119.9 1.0 copy.65
  121.0 1.4 fusion.133
  123.5 7.9 %convolution_bitcast_fusion.8 = f32[192,128]{1,0:T(8,128)S(1)} fusion(f32[8,132,192]{2,1,0:T(8,128)} %convolution_bitcast_fusion, f32[8,132,192]{2,1,0:T(8,128)S(1)} %get-tuple-element.27, f32[8,132]{1,0:T(8,128)S(1)} %log_add_fusion, bf16[132,8,128]{2,1,0:T(8,128)(2,1)S(1)} %slice.128), kind=kOutput, calls=%fused_computation.48 | convolution fusion | flops 53325024 | bytes 1994880 | tf_op jit(solution)/shard_map/gmn,mgd->nd/dot_general | solution.py:97
  131.5 7.5 %fusion.31 = bf16[132,8,128]{2,0,1:T(8,128)(2,1)S(1)} fusion(f32[8,132,192]{2,1,0:T(8,128)} %convolution_bitcast_fusion, f32[8,132,192]{2,1,0:T(8,128)S(1)} %get-tuple-element.27, f32[8,132]{1,0:T(8,128)S(1)} %log_add_fusion, bf16[192,512]{1,0:T(8,128)(2,1)} %copy-done.8), kind=kOutput, calls=%fused_computation.43 | convolution fusion | flops 53460192 | bytes 4792320 | tf_op jit(solution)/shard_map/gmn,nd->mgd/dot_general | solution.py:92
  139.8 1.0 slice.116
  140.9 0.7 slice.152
  142.3 61.4 %all-reduce.4 = bf16[64,1024]{1,0:T(8,128)(2,1)S(1)} all-reduce(f32[64,1024]{1,0:T(8,128)S(1)} %fusion.88), channel_id=2, replica_groups=mesh['grp'=2,'seq'=16] {'seq'}, use_global_device_ids=true, to_apply=%region_17.18.clone | all-reduce | flops 65536 | bytes 393216
  (93 shorter events, 10.9 us)
Async XLA Ops:
  0.6 51.5 %copy-start.9 = (bf16[4,4096]{1,0:T(4,128)(2,1)S(1)}, bf16[4,4096]{1,0:T(4,128)(2,1)}, u32[]{:S(2)}) copy-start(bf16[4,4096]{1,0:T(4,128)(2,1)} %param.18) | copy-start | bytes 98308
  0.6 51.5 %copy-start.2 = (bf16[128,4096]{1,0:T(8,128)(2,1)S(1)}, bf16[128,4096]{1,0:T(8,128)(2,1)}, u32[]{:S(2)}) copy-start(bf16[128,4096]{1,0:T(8,128)(2,1)} %param.17) | copy-start | bytes 3145732
  52.1 18.9 %copy-start.8 = (bf16[192,512]{1,0:T(8,128)(2,1)}, bf16[192,512]{1,0:T(8,128)(2,1)S(1)}, u32[]{:S(2)}) copy-start(bf16[192,512]{1,0:T(8,128)(2,1)S(1)} %constant_dynamic-update-slice_fusion) | copy-start | bytes 589828
  55.5 2.7 %copy-start.3 = (bf16[128,4096]{1,0:T(8,128)(2,1)S(1)}, bf16[128,4096]{1,0:T(8,128)(2,1)}, u32[]{:S(2)}) copy-start(bf16[128,4096]{1,0:T(8,128)(2,1)} %param.11) | copy-start | bytes 3145732
  58.2 0.8 copy-start.10
  78.5 1.0 copy-start.1
  98.8 1.2 copy-start
  139.1 1.7 copy-start.5
  139.1 1.7 copy-start.6
  139.2 1.7 copy-start.7
  139.8 1.1 copy-start.4
where the time goes:
time: 205 us; the launch traced here: 204 us
  blocking collectives  103 us (50%)
  matrix products  77.9 us (38%)
  local copies, waits for them, and re-layouts  13.4 us (7%)
  other arithmetic  8.29 us (4%)
    unnamed x1, blocking collectives  61.4 us
    dot_general x4, matrix products, slot_pass(): jnp.einsum('gmn,mgd->nd', score_grad, q_head, preferred_element_type=jnp....  33.5 us
    dot_general x4, matrix products, slot_pass(): jnp.einsum('gmn,nd->mgd', score_grad, k_head, preferred_element_type=jnp....  31.3 us
    all_gather x1, blocking collectives, local(): lax.all_gather(beacon_keys, 'seq', axis=0, tiled=True)  23.5 us
    all_gather x1, blocking collectives, local(): lax.all_gather(beacon_values, 'seq', axis=0, tiled=True)  17.9 us
    dot_general x4, matrix products, slot_pass(): jnp.einsum('mgd,nd->gmn', g_head, v_head, preferred_element_type=jnp.floa...  5.29 us
    dot_general x4, matrix products, slot_pass(): jnp.einsum('mgd,nd->gmn', q_head, k_head, preferred_element_type=jnp.floa...  4.72 us

commit v1 on v0

v1 whole, which is shorter than its diff:
```python
import functools

import jax
import jax.numpy as jnp
from jax import lax
from jax.experimental import pallas as pl
from jax.experimental.pallas import tpu as pltpu
from jax.sharding import PartitionSpec as P

HEADS = 32
KV = 4
D = 128
SPAN = 128
B = 4
GROUP = HEADS // KV
CHUNK = 256
WIDE = GROUP * SPAN
SCALE = D ** (-0.5)
EXP2 = SCALE * 1.4426950408889634
LOW = -1e30
F32 = jnp.float32
BF16 = jnp.bfloat16
MESH = pl.DeviceIdType.MESH


def nt(a, b):
    return lax.dot_general(a, b, (((1,), (1,)), ((), ())), preferred_element_type=F32)


def nn(a, b):
    return lax.dot_general(a, b, (((1,), (0,)), ((), ())), preferred_element_type=F32)


def tn(a, b):
    return lax.dot_general(a, b, (((0,), (0,)), ((), ())), preferred_element_type=F32)


def each(n, body):
    if n <= 16:
        for d in range(1, n):
            body(d)
    else:
        lax.fori_loop(1, n, lambda d, c: (body(d), c)[1], 0)


def stack_heads(ref, kv, first, count):
    low = (kv * GROUP + first) * D
    return jnp.concatenate([ref[:, low + i * D : low + (i + 1) * D] for i in range(count)], axis=0)


def kernel(
    n,
    rq, bq, rk, rv, bk, bv, rg, bg, ss, bc, fs,
    rq_out, bq_out, rk_out, rv_out, bk_out, bv_out,
    q, g, k, v, bqs, bgs, bks, bvs,
    qx, gx, msg, gat, kb, vb,
    p_r, dp_r, p_x, dp_x, stat,
    a_all, ds_all, sbuf, rbuf, oq, obq, ok, ov, obk, obv,
    local_sem, out_sem, ag_send, ag_recv, rs_send, rs_recv,
):
    me = lax.axis_index("seq")
    rows = n * B

    small = [
        pltpu.make_async_copy(a, b, local_sem.at[i])
        for i, (a, b) in enumerate([(bk, bks), (bv, bvs), (rk, k), (rv, v), (bq, bqs), (bg, bgs)])
    ]
    for c in small:
        c.start()
    large = []
    for kv in range(KV):
        cols = pl.ds(kv * WIDE, WIDE)
        cq = pltpu.make_async_copy(rq.at[:, cols], q.at[:, cols], local_sem.at[6 + 2 * kv])
        cg = pltpu.make_async_copy(rg.at[:, cols], g.at[:, cols], local_sem.at[7 + 2 * kv])
        cq.start()
        cg.start()
        large.append((cq, cg))

    barrier = pltpu.get_barrier_semaphore()

    def greet(d):
        pl.semaphore_signal(
            barrier, inc=1, device_id={"seq": lax.rem(me + d, n)}, device_id_type=MESH
        )

    each(n, greet)

    small[0].wait()
    small[1].wait()
    bk32 = bks[...].astype(F32)
    bv32 = bvs[...].astype(F32)
    for kv in range(KV):
        msg[kv * B : (kv + 1) * B, :] = bk32[:, kv * D : (kv + 1) * D]
        msg[(KV + kv) * B : (KV + kv + 1) * B, :] = bv32[:, kv * D : (kv + 1) * D]
    gat[0] = msg[...].astype(BF16)

    pl.semaphore_wait(barrier, n - 1)

    def gather_copy(d):
        return pltpu.make_async_remote_copy(
            src_ref=gat.at[0],
            dst_ref=gat.at[d],
            send_sem=ag_send,
            recv_sem=ag_recv,
            device_id={"seq": lax.rem(me + d, n)},
            device_id_type=MESH,
        )

    each(n, lambda d: gather_copy(d).start())

    ssf, bcf, fsf = ss[...].astype(F32), bc[...].astype(F32), fs[...].astype(F32)
    col = lax.broadcasted_iota(jnp.int32, (1, n), 1)
    colf = col.astype(F32)
    own_span = jnp.sum(jnp.where(col == me, ssf, 0.0), axis=1, keepdims=True)
    own_first = jnp.sum(jnp.where(colf == own_span, fsf, 0.0), axis=1, keepdims=True)
    own_count = jnp.sum(jnp.where(colf == own_span, bcf, 0.0), axis=1, keepdims=True)
    row = lax.broadcasted_iota(jnp.int32, (rows, n), 0)
    back = me - row // B
    slot = jnp.where(back < 0, back + n, back)
    rcol = lax.broadcasted_iota(jnp.int32, (rows, n), 1)
    key_span = jnp.sum(jnp.where(slot == rcol, ssf, 0.0), axis=1, keepdims=True)
    key_count = jnp.sum(
        jnp.where(rcol.astype(F32) == key_span, bcf, 0.0), axis=1, keepdims=True
    )
    wide_row = lax.broadcasted_iota(jnp.int32, (rows, D), 0)
    wide_lane = lax.broadcasted_iota(jnp.int32, (rows, D), 1)
    beacon = wide_row % B
    live = beacon.astype(F32) < key_count
    earlier = (own_first <= key_span) & (key_span < own_span) & live
    own_beacons = (wide_row < B) & (beacon <= wide_lane % B) & live
    see_raw = jnp.where(earlier, 0.0, LOW)
    see_beacon = jnp.where(earlier | own_beacons, 0.0, LOW)
    causal = lax.broadcasted_iota(jnp.int32, (SPAN, SPAN), 0) <= lax.broadcasted_iota(
        jnp.int32, (SPAN, SPAN), 1
    )
    causal2 = jnp.concatenate([causal] * (CHUNK // SPAN), axis=1)

    for c in small[2:]:
        c.wait()
    bq32 = bqs[...].astype(F32)
    bg32 = jnp.where(
        lax.broadcasted_iota(jnp.int32, (B, 1), 0).astype(F32) < own_count,
        bgs[...].astype(F32),
        0.0,
    )
    for h in range(HEADS):
        qx[h * B : (h + 1) * B, :] = bq32[:, h * D : (h + 1) * D]
        gx[h * B : (h + 1) * B, :] = bg32[:, h * D : (h + 1) * D]
    qxb = qx[...].astype(BF16)
    gxb = gx[...].astype(BF16)
    group_lane = lax.broadcasted_iota(jnp.int32, (1, D), 1) // (GROUP * B)

    def own_keys(kv):
        return k[:, kv * D : (kv + 1) * D], v[:, kv * D : (kv + 1) * D]

    def pick(parts):
        out = parts[0]
        for kv in range(1, KV):
            out = jnp.where(group_lane == kv, parts[kv], out)
        return out

    s = pick([nt(own_keys(kv)[0], qxb) for kv in range(KV)])
    dp = pick([nt(own_keys(kv)[1], gxb) for kv in range(KV)])
    m = jnp.max(s, axis=0, keepdims=True)
    p = jnp.exp2((s - m) * EXP2)
    p_x[...] = p
    dp_x[...] = dp
    x_stat = (m, jnp.sum(p, axis=0, keepdims=True), jnp.sum(p * dp, axis=0, keepdims=True))

    per = CHUNK // SPAN
    for kv in range(KV):
        for c in large[kv]:
            c.wait()
        kr, vr = own_keys(kv)
        for c in range(GROUP // per):
            cols = slice(c * CHUNK, (c + 1) * CHUNK)
            s = nt(kr, stack_heads(q, kv, c * per, per))
            dp = nt(vr, stack_heads(g, kv, c * per, per))
            s = jnp.where(causal2, s, LOW)
            m = jnp.max(s, axis=0, keepdims=True)
            p = jnp.exp2((s - m) * EXP2)
            p_r[kv, :, cols] = p
            dp_r[kv, :, cols] = dp
            stat[kv, 0:1, cols] = m
            stat[kv, 1:2, cols] = jnp.sum(p, axis=0, keepdims=True)
            stat[kv, 2:3, cols] = jnp.sum(p * dp, axis=0, keepdims=True)

    pltpu.make_async_copy(gat.at[pl.ds(1, n - 1)], gat.at[pl.ds(1, n - 1)], ag_recv).wait()
    top = lax.broadcasted_iota(jnp.int32, (1, 8, D), 1) < B
    got = gat[...].astype(F32).reshape(n // 2, 2, 2 * KV * B // 8, 8, D)
    for t in range(2 * KV * B // 8):
        even, odd = got[:, 0, t], got[:, 1, t]
        lo = jnp.where(top, even, pltpu.roll(odd, B, 1))
        hi = jnp.where(top, pltpu.roll(even, B, 1), odd)
        into = kb if t < KV // 2 else vb
        kv = 2 * (t % (KV // 2))
        into[kv] = lo.reshape(rows, D).astype(BF16)
        into[kv + 1] = hi.reshape(rows, D).astype(BF16)

    def beacon_part(s, dp, see, m1, l1, u1):
        s = s + see
        m = jnp.maximum(m1, jnp.max(s, axis=0, keepdims=True))
        p = jnp.exp2((s - m) * EXP2)
        alpha = jnp.exp2((m1 - m) * EXP2)
        total = alpha * l1 + jnp.sum(p, axis=0, keepdims=True)
        inverse = 1.0 / total
        delta = (alpha * u1 + jnp.sum(p * dp, axis=0, keepdims=True)) * inverse
        a = p * inverse
        ds = a * (dp - delta) * SCALE
        return a, ds, alpha * inverse, delta

    a, ds, x_factor, x_delta = beacon_part(
        pick([nt(kb[kv], qxb) for kv in range(KV)]),
        pick([nt(vb[kv], gxb) for kv in range(KV)]),
        see_beacon,
        *x_stat,
    )
    for kv in range(KV):
        a_all[kv, :rows, WIDE:] = jnp.where(group_lane == kv, a, 0.0).astype(BF16)
        ds_all[kv, :rows, WIDE:] = jnp.where(group_lane == kv, ds, 0.0).astype(BF16)
    see2 = jnp.concatenate([see_raw] * per, axis=1)

    def sum_copy(pair, d):
        owner = me - d
        owner = jnp.where(owner < 0, owner + n, owner)
        return pltpu.make_async_remote_copy(
            src_ref=sbuf.at[pair, d],
            dst_ref=rbuf.at[pair, d],
            send_sem=rs_send.at[pair],
            recv_sem=rs_recv.at[pair],
            device_id={"seq": owner},
            device_id_type=MESH,
        )

    for pair in range(KV // 2):
        tiles = []
        for kv in (2 * pair, 2 * pair + 1):
            for c in range(GROUP // per):
                cols = slice(c * CHUNK, (c + 1) * CHUNK)
                a, ds, factor, delta = beacon_part(
                    nt(kb[kv], stack_heads(q, kv, c * per, per)),
                    nt(vb[kv], stack_heads(g, kv, c * per, per)),
                    see2,
                    stat[kv, 0:1, cols],
                    stat[kv, 1:2, cols],
                    stat[kv, 2:3, cols],
                )
                a_all[kv, :rows, cols] = a.astype(BF16)
                ds_all[kv, :rows, cols] = ds.astype(BF16)
                stat[kv, 3:4, cols] = factor
                stat[kv, 4:5, cols] = delta
            q_rows = jnp.concatenate([stack_heads(q, kv, 0, GROUP), qxb], axis=0)
            g_rows = jnp.concatenate([stack_heads(g, kv, 0, GROUP), gxb], axis=0)
            dk = nn(ds_all[kv, :rows, :], q_rows).reshape(n // 2, 8, D)
            dv = nn(a_all[kv, :rows, :], g_rows).reshape(n // 2, 8, D)
            even = jnp.where(top, dk, pltpu.roll(dv, B, 1))
            odd = jnp.where(top, pltpu.roll(dk, B, 1), dv)
            tiles.append(jnp.stack([even, odd], axis=1).reshape(n, 8, D))
        both = jnp.concatenate(tiles, axis=1).astype(BF16)
        sbuf[pair] = both
        rbuf[pair, 0] = both[0]
        each(n, lambda d: sum_copy(pair, d).start())

    out_copies = []
    a = p_x[...] * x_factor
    ds = a * (dp_x[...] - x_delta) * SCALE
    dqx = None
    for kv in range(KV):
        a_all[kv, rows:, WIDE:] = jnp.where(group_lane == kv, a, 0.0).astype(BF16)
        ds_all[kv, rows:, WIDE:] = jnp.where(group_lane == kv, ds, 0.0).astype(BF16)
    for kv in range(KV):
        kr, vr = own_keys(kv)
        keys = jnp.concatenate([kb[kv], kr], axis=0)
        for c in range(GROUP // per):
            cols = slice(c * CHUNK, (c + 1) * CHUNK)
            a = p_r[kv, :, cols] * stat[kv, 3:4, cols]
            ds = a * (dp_r[kv, :, cols] - stat[kv, 4:5, cols]) * SCALE
            a_all[kv, rows:, cols] = a.astype(BF16)
            ds_all[kv, rows:, cols] = ds.astype(BF16)
            dq = tn(ds_all[kv, :, cols], keys).astype(BF16)
            for i in range(per):
                low = (kv * GROUP + c * per + i) * D
                oq[:, low : low + D] = dq[i * SPAN : (i + 1) * SPAN]
        cols = pl.ds(kv * WIDE, WIDE)
        oc = pltpu.make_async_copy(oq.at[:, cols], rq_out.at[:, cols], out_sem.at[kv])
        oc.start()
        out_copies.append(oc)
        term = tn(ds_all[kv, :, WIDE:], keys)
        dqx = term if dqx is None else dqx + term
        q_rows = jnp.concatenate([stack_heads(q, kv, 0, GROUP), qxb], axis=0)
        g_rows = jnp.concatenate([stack_heads(g, kv, 0, GROUP), gxb], axis=0)
        ok[:, kv * D : (kv + 1) * D] = nn(ds_all[kv, rows:, :], q_rows).astype(BF16)
        ov[:, kv * D : (kv + 1) * D] = nn(a_all[kv, rows:, :], g_rows).astype(BF16)
    obq[...] = jnp.concatenate(
        [dqx[h * B : (h + 1) * B] for h in range(HEADS)], axis=1
    ).astype(BF16)
    for i, (a, b) in enumerate([(ok, rk_out), (ov, rv_out), (obq, bq_out)]):
        oc = pltpu.make_async_copy(a, b, out_sem.at[KV + i])
        oc.start()
        out_copies.append(oc)

    dk_parts, dv_parts = [], []
    for pair in range(KV // 2):
        arrived = rbuf.at[pair, pl.ds(1, n - 1)]
        pltpu.make_async_copy(arrived, arrived, rs_recv.at[pair]).wait()
        total = jnp.sum(rbuf[pair].astype(F32), axis=0)
        for i in range(2):
            dk_parts.append(total[8 * i : 8 * i + B])
            dv_parts.append(total[8 * i + B : 8 * i + 8])
    obk[...] = jnp.concatenate(dk_parts, axis=1).astype(BF16)
    obv[...] = jnp.concatenate(dv_parts, axis=1).astype(BF16)
    for i, (a, b) in enumerate([(obk, bk_out), (obv, bv_out)]):
        oc = pltpu.make_async_copy(a, b, out_sem.at[KV + 3 + i])
        oc.start()
        out_copies.append(oc)
    pltpu.make_async_copy(gat.at[pl.ds(1, n - 1)], gat.at[pl.ds(1, n - 1)], ag_send).wait()
    for pair in range(KV // 2):
        left = sbuf.at[pair, pl.ds(1, n - 1)]
        pltpu.make_async_copy(left, left, rs_send.at[pair]).wait()
    for oc in out_copies:
        oc.wait()


def local(n, *args):
    rows = n * B
    keys = rows + SPAN
    rq, bq, rk, rv, bk, bv, rg, bg, ss, bc, fs = args
    out_shape = [jax.ShapeDtypeStruct(x.shape, BF16) for x in (rq, bq, rk, rv, bk, bv)]
    vm = pltpu.VMEM
    any_spec = pl.BlockSpec(memory_space=pl.ANY)
    vmem_spec = pl.BlockSpec(memory_space=pltpu.VMEM)
    scratch = [
        vm(rq.shape, BF16), vm(rg.shape, BF16), vm(rk.shape, BF16), vm(rv.shape, BF16),
        vm(bq.shape, BF16), vm(bg.shape, BF16), vm(bk.shape, BF16), vm(bv.shape, BF16),
        vm((HEADS * B, D), F32), vm((HEADS * B, D), F32),
        vm((2 * KV * B, D), F32), vm((n, 2 * KV * B, D), BF16),
        vm((KV, rows, D), BF16), vm((KV, rows, D), BF16),
        vm((KV, SPAN, WIDE), F32), vm((KV, SPAN, WIDE), F32),
        vm((SPAN, D), F32), vm((SPAN, D), F32), vm((KV, 8, WIDE), F32),
        vm((KV, keys, WIDE + D), BF16), vm((KV, keys, WIDE + D), BF16),
        vm((KV // 2, n, 16, D), BF16), vm((KV // 2, n, 16, D), BF16),
        vm(rq.shape, BF16), vm(bq.shape, BF16), vm(rk.shape, BF16), vm(rv.shape, BF16),
        vm(bk.shape, BF16), vm(bv.shape, BF16),
        pltpu.SemaphoreType.DMA((6 + 2 * KV,)), pltpu.SemaphoreType.DMA((KV + 5,)),
        pltpu.SemaphoreType.DMA, pltpu.SemaphoreType.DMA,
        pltpu.SemaphoreType.DMA((KV // 2,)), pltpu.SemaphoreType.DMA((KV // 2,)),
    ]
    return pl.pallas_call(
        functools.partial(kernel, n),
        out_shape=out_shape,
        in_specs=[any_spec] * 8 + [vmem_spec] * 3,
        out_specs=[any_spec] * 6,
        scratch_shapes=scratch,
        compiler_params=pltpu.CompilerParams(
            collective_id=0, has_side_effects=True, vmem_limit_bytes=50 * 2**20
        ),
    )(rq, bq, rk, rv, bk, bv, rg, bg, ss.reshape(1, n), bc.reshape(1, n), fs.reshape(1, n))


def solution(mesh):
    sharded = P(("grp", "seq"), None)
    return jax.shard_map(
        functools.partial(local, mesh.shape["seq"]),
        mesh=mesh,
        in_specs=(sharded,) * 8 + (P("grp"),) * 3,
        out_specs=(sharded,) * 6,
        check_vma=False,
    )
```

time: 205 us -> 31.2 us (0.15)
  blocking collectives: 103 us -> 0 us
  matrix products: 77.9 us -> 0 us
  Pallas kernels: 0 us -> 18.9 us
  other arithmetic: 8.29 us -> 0 us
  local copies, waits for them, and re-layouts: 13.4 us -> 11.2 us
    dot_general x20 -> x0, matrix products: 77.9 us -> none  [the longest x4 33.5 us: slot_pass(): jnp.einsum('gmn,mgd->nd', score_grad, q_head, preferred_element_type=jnp....]
    unnamed x1 -> x0, blocking collectives: 61.4 us -> none
    all_gather x2 -> x0, blocking collectives: 41.4 us -> none  [the longest x1 23.5 us: local(): lax.all_gather(beacon_keys, 'seq', axis=0, tiled=True)]
    pallas_call x0 -> x1, Pallas kernels: none -> 18.9 us  [local(): pl.pallas_call(functools.partial(kernel, n), out_shape=out_shape, in_spec...]
    unnamed x47 -> x28, local copies, waits for them, and re-layouts: 3.57 us -> 11.2 us
    reduce_sum x7 -> x0, other arithmetic: 5.15 us -> none  [the longest x4 2.26 us: slot_pass(): row_total = jnp.sum(jnp.exp(scores - row_max), axis=-1, keepdims=True)]
    slice x7 -> x0, local copies, waits for them, and re-layouts: 3.76 us -> none  [the longest x1 1.04 us: local(): raw_query_parts.append(query_grad[:SPAN])]
    transpose x4 -> x0, local copies, waits for them, and re-layouts: 2.1 us -> none  [slot_pass(): jnp.einsum('gmn,nd->mgd', score_grad, k_head, preferred_element_type=jnp....]
where the time goes in v1:
time: 31.2 us; the launch traced here: 30.8 us
  Pallas kernels  18.9 us (61%)
  local copies, waits for them, and re-layouts  11.2 us (36%)
  between operations  0.69 us (2%)
    pallas_call x1, Pallas kernels, local(): pl.pallas_call(functools.partial(kernel, n), out_shape=out_shape, in_spec...  18.9 us
    unnamed x28, local copies, waits for them, and re-layouts  11.2 us

profile of v1, /device:TPU:0, one launch (start us, length us, event | category | flops | bytes accessed | tf_op | source)
XLA Modules:
  0.0 30.8 jit_solution(15995003661812081132)
XLA Ops:
  0.6 0.0 copy-start.6
  0.6 0.0 copy-start.8
  0.7 0.0 copy-start.9
  0.7 0.0 copy-start.10
  0.7 0.6 %copy-done.6 = bf16[4,512]{1,0:T(4,128)(2,1)S(1)} copy-done((bf16[4,512]{1,0:T(4,128)(2,1)S(1)}, bf16[4,512]{1,0:T(4,128)(2,1)}, u32[]{:S(2)}) %copy-start.6) | copy-done | bytes 4120
  1.3 0.0 copy-done.8
  1.3 0.0 copy-done.9
  1.3 0.0 copy-done.10
  1.3 0.0 copy-start
  1.3 1.2 %copy-done = bf16[128,4096]{1,0:T(8,128)(2,1)S(1)} copy-done((bf16[128,4096]{1,0:T(8,128)(2,1)S(1)}, bf16[128,4096]{1,0:T(8,128)(2,1)}, u32[]{:S(2)}) %copy-start) | copy-done | bytes 1048600
  2.6 0.0 copy-start.1
  2.6 1.2 %copy-done.1 = bf16[128,4096]{1,0:T(8,128)(2,1)S(1)} copy-done((bf16[128,4096]{1,0:T(8,128)(2,1)S(1)}, bf16[128,4096]{1,0:T(8,128)(2,1)}, u32[]{:S(2)}) %copy-start.1) | copy-done | bytes 1048600
  3.8 0.0 copy-start.2
  3.8 0.9 %copy-done.2 = bf16[128,512]{1,0:T(8,128)(2,1)S(1)} copy-done((bf16[128,512]{1,0:T(8,128)(2,1)S(1)}, bf16[128,512]{1,0:T(8,128)(2,1)}, u32[]{:S(2)}) %copy-start.2) | copy-done | bytes 131096
  4.7 0.0 copy-start.3
  4.7 0.9 %copy-done.3 = bf16[128,512]{1,0:T(8,128)(2,1)S(1)} copy-done((bf16[128,512]{1,0:T(8,128)(2,1)S(1)}, bf16[128,512]{1,0:T(8,128)(2,1)}, u32[]{:S(2)}) %copy-start.3) | copy-done | bytes 131096
  5.6 0.0 copy-start.4
  5.6 0.8 %copy-done.4 = bf16[4,4096]{1,0:T(4,128)(2,1)S(1)} copy-done((bf16[4,4096]{1,0:T(4,128)(2,1)S(1)}, bf16[4,4096]{1,0:T(4,128)(2,1)}, u32[]{:S(2)}) %copy-start.4) | copy-done | bytes 32792
  6.4 0.0 copy-start.5
  6.4 0.8 %copy-done.5 = bf16[4,4096]{1,0:T(4,128)(2,1)S(1)} copy-done((bf16[4,4096]{1,0:T(4,128)(2,1)S(1)}, bf16[4,4096]{1,0:T(4,128)(2,1)}, u32[]{:S(2)}) %copy-start.5) | copy-done | bytes 32792
  7.1 0.0 copy-start.7
  7.1 0.7 %copy-done.7 = bf16[4,512]{1,0:T(4,128)(2,1)S(1)} copy-done((bf16[4,512]{1,0:T(4,128)(2,1)S(1)}, bf16[4,512]{1,0:T(4,128)(2,1)}, u32[]{:S(2)}) %copy-start.7) | copy-done | bytes 4120
  7.8 18.9 %shard_map.154 = (bf16[128,4096]{1,0:T(8,128)(2,1)S(1)}, bf16[4,4096]{1,0:T(4,128)(2,1)S(1)}, bf16[128,512]{1,0:T(8,128)(2,1)S(1)}, bf16[128,512]{1,0:T(8,128)(2...) custom-call(bf16[128,4096]{1,0:T(8,128)(2,1)S(1)} %copy-done, bf16[4,4096]{1,0:T(4,128)(2,1)S(1)} %copy-done.4, ...), custom_call_target="tpu_custom_call" | custom-call | tf_op jit(solution)/shard_map/pallas_call | solution.py:348
  26.7 1.0 %copy.23 = bf16[128,4096]{1,0:T(8,128)(2,1)} copy(bf16[128,4096]{1,0:T(8,128)(2,1)S(1)} %get-tuple-element.12) | data formatting | bytes 2097152
  27.7 0.6 %copy.24 = bf16[4,4096]{1,0:T(4,128)(2,1)} copy(bf16[4,4096]{1,0:T(4,128)(2,1)S(1)} %get-tuple-element.13) | data formatting | bytes 65536
  28.3 0.7 %copy.25 = bf16[128,512]{1,0:T(8,128)(2,1)} copy(bf16[128,512]{1,0:T(8,128)(2,1)S(1)} %get-tuple-element.14) | data formatting | bytes 262144
  29.0 0.7 %copy.26 = bf16[128,512]{1,0:T(8,128)(2,1)} copy(bf16[128,512]{1,0:T(8,128)(2,1)S(1)} %get-tuple-element.15) | data formatting | bytes 262144
  29.6 0.6 %copy.27 = bf16[4,512]{1,0:T(4,128)(2,1)} copy(bf16[4,512]{1,0:T(4,128)(2,1)S(1)} %get-tuple-element.16) | data formatting | bytes 8192
  30.2 0.6 %copy.28 = bf16[4,512]{1,0:T(4,128)(2,1)} copy(bf16[4,512]{1,0:T(4,128)(2,1)S(1)} %get-tuple-element.17) | data formatting | bytes 8192
Async XLA Ops:
  0.6 0.7 %copy-start.6 = (bf16[4,512]{1,0:T(4,128)(2,1)S(1)}, bf16[4,512]{1,0:T(4,128)(2,1)}, u32[]{:S(2)}) copy-start(bf16[4,512]{1,0:T(4,128)(2,1)} %bk.1) | copy-start | bytes 12292
  0.6 0.7 %copy-start.8 = (s32[16]{0:T(128)S(1)}, s32[16]{0:T(128)}, u32[]{:S(2)}) copy-start(s32[16]{0:T(128)} %param.19) | copy-start | bytes 196
  0.7 0.7 %copy-start.9 = (s32[16]{0:T(128)S(1)}, s32[16]{0:T(128)}, u32[]{:S(2)}) copy-start(s32[16]{0:T(128)} %param.20) | copy-start | bytes 196
  0.7 0.7 %copy-start.10 = (s32[16]{0:T(128)S(1)}, s32[16]{0:T(128)}, u32[]{:S(2)}) copy-start(s32[16]{0:T(128)} %param.21) | copy-start | bytes 196
  1.3 1.2 %copy-start = (bf16[128,4096]{1,0:T(8,128)(2,1)S(1)}, bf16[128,4096]{1,0:T(8,128)(2,1)}, u32[]{:S(2)}) copy-start(bf16[128,4096]{1,0:T(8,128)(2,1)} %rq.1) | copy-start | bytes 3145732
  2.6 1.2 %copy-start.1 = (bf16[128,4096]{1,0:T(8,128)(2,1)S(1)}, bf16[128,4096]{1,0:T(8,128)(2,1)}, u32[]{:S(2)}) copy-start(bf16[128,4096]{1,0:T(8,128)(2,1)} %rg.1) | copy-start | bytes 3145732
  3.8 0.9 %copy-start.2 = (bf16[128,512]{1,0:T(8,128)(2,1)S(1)}, bf16[128,512]{1,0:T(8,128)(2,1)}, u32[]{:S(2)}) copy-start(bf16[128,512]{1,0:T(8,128)(2,1)} %rk.1) | copy-start | bytes 393220
  4.7 0.9 %copy-start.3 = (bf16[128,512]{1,0:T(8,128)(2,1)S(1)}, bf16[128,512]{1,0:T(8,128)(2,1)}, u32[]{:S(2)}) copy-start(bf16[128,512]{1,0:T(8,128)(2,1)} %rv.1) | copy-start | bytes 393220
  5.6 0.8 %copy-start.4 = (bf16[4,4096]{1,0:T(4,128)(2,1)S(1)}, bf16[4,4096]{1,0:T(4,128)(2,1)}, u32[]{:S(2)}) copy-start(bf16[4,4096]{1,0:T(4,128)(2,1)} %bq.1) | copy-start | bytes 98308
  6.4 0.8 %copy-start.5 = (bf16[4,4096]{1,0:T(4,128)(2,1)S(1)}, bf16[4,4096]{1,0:T(4,128)(2,1)}, u32[]{:S(2)}) copy-start(bf16[4,4096]{1,0:T(4,128)(2,1)} %bg.1) | copy-start | bytes 98308
  7.1 0.7 %copy-start.7 = (bf16[4,512]{1,0:T(4,128)(2,1)S(1)}, bf16[4,512]{1,0:T(4,128)(2,1)}, u32[]{:S(2)}) copy-start(bf16[4,512]{1,0:T(4,128)(2,1)} %bv.1) | copy-start | bytes 12292

commit v2 on v1

--- a/solution.py
+++ b/solution.py
@@ -20,6 +20,7 @@
 LOW = -1e30
 F32 = jnp.float32
 BF16 = jnp.bfloat16
+VMEM_LIMIT = 48 * 2**20
 MESH = pl.DeviceIdType.MESH
 
 
@@ -51,30 +52,15 @@
 def kernel(
     n,
     rq, bq, rk, rv, bk, bv, rg, bg, ss, bc, fs,
-    rq_out, bq_out, rk_out, rv_out, bk_out, bv_out,
-    q, g, k, v, bqs, bgs, bks, bvs,
+    oq, obq, ok, ov, obk, obv,
+    q, g, k, v, bqs, bgs, bks, bvs, sss, bcs, fss,
     qx, gx, msg, gat, kb, vb,
     p_r, dp_r, p_x, dp_x, stat,
-    a_all, ds_all, sbuf, rbuf, oq, obq, ok, ov, obk, obv,
-    local_sem, out_sem, ag_send, ag_recv, rs_send, rs_recv,
+    a_all, ds_all, sbuf, rbuf,
+    local_sem, ag_send, ag_recv, rs_send, rs_recv,
 ):
     me = lax.axis_index("seq")
     rows = n * B
-
-    small = [
-        pltpu.make_async_copy(a, b, local_sem.at[i])
-        for i, (a, b) in enumerate([(bk, bks), (bv, bvs), (rk, k), (rv, v), (bq, bqs), (bg, bgs)])
-    ]
-    for c in small:
-        c.start()
-    large = []
-    for kv in range(KV):
-        cols = pl.ds(kv * WIDE, WIDE)
-        cq = pltpu.make_async_copy(rq.at[:, cols], q.at[:, cols], local_sem.at[6 + 2 * kv])
-        cg = pltpu.make_async_copy(rg.at[:, cols], g.at[:, cols], local_sem.at[7 + 2 * kv])
-        cq.start()
-        cg.start()
-        large.append((cq, cg))
 
     barrier = pltpu.get_barrier_semaphore()
 
@@ -84,6 +70,14 @@
         )
 
     each(n, greet)
+
+    pairs = [
+        (bk, bks), (bv, bvs), (ss, sss), (bc, bcs), (fs, fss),
+        (rk, k), (rv, v), (bq, bqs), (bg, bgs),
+    ]
+    small = [pltpu.make_async_copy(a, b, local_sem.at[i]) for i, (a, b) in enumerate(pairs)]
+    small[0].start()
+    small[1].start()
 
     small[0].wait()
     small[1].wait()
@@ -108,7 +102,21 @@
 
     each(n, lambda d: gather_copy(d).start())
 
-    ssf, bcf, fsf = ss[...].astype(F32), bc[...].astype(F32), fs[...].astype(F32)
+    for c in small[2:]:
+        c.start()
+    large = []
+    for kv in range(KV):
+        cols = pl.ds(kv * WIDE, WIDE)
+        first = len(pairs) + 2 * kv
+        cq = pltpu.make_async_copy(rq.at[:, cols], q.at[:, cols], local_sem.at[first])
+        cg = pltpu.make_async_copy(rg.at[:, cols], g.at[:, cols], local_sem.at[first + 1])
+        cq.start()
+        cg.start()
+        large.append((cq, cg))
+    for c in small[2:]:
+        c.wait()
+
+    ssf, bcf, fsf = sss[...].astype(F32), bcs[...].astype(F32), fss[...].astype(F32)
     col = lax.broadcasted_iota(jnp.int32, (1, n), 1)
     colf = col.astype(F32)
     own_span = jnp.sum(jnp.where(col == me, ssf, 0.0), axis=1, keepdims=True)
@@ -135,8 +143,6 @@
     )
     causal2 = jnp.concatenate([causal] * (CHUNK // SPAN), axis=1)
 
-    for c in small[2:]:
-        c.wait()
     bq32 = bqs[...].astype(F32)
     bg32 = jnp.where(
         lax.broadcasted_iota(jnp.int32, (B, 1), 0).astype(F32) < own_count,
@@ -261,7 +267,6 @@
         rbuf[pair, 0] = both[0]
         each(n, lambda d: sum_copy(pair, d).start())
 
-    out_copies = []
     a = p_x[...] * x_factor
     ds = a * (dp_x[...] - x_delta) * SCALE
     dqx = None
@@ -281,10 +286,6 @@
             for i in range(per):
                 low = (kv * GROUP + c * per + i) * D
                 oq[:, low : low + D] = dq[i * SPAN : (i + 1) * SPAN]
-        cols = pl.ds(kv * WIDE, WIDE)
-        oc = pltpu.make_async_copy(oq.at[:, cols], rq_out.at[:, cols], out_sem.at[kv])
-        oc.start()
-        out_copies.append(oc)
         term = tn(ds_all[kv, :, WIDE:], keys)
         dqx = term if dqx is None else dqx + term
         q_rows = jnp.concatenate([stack_heads(q, kv, 0, GROUP), qxb], axis=0)
@@ -294,10 +295,6 @@
     obq[...] = jnp.concatenate(
         [dqx[h * B : (h + 1) * B] for h in range(HEADS)], axis=1
     ).astype(BF16)
-    for i, (a, b) in enumerate([(ok, rk_out), (ov, rv_out), (obq, bq_out)]):
-        oc = pltpu.make_async_copy(a, b, out_sem.at[KV + i])
-        oc.start()
-        out_copies.append(oc)
 
     dk_parts, dv_parts = [], []
     for pair in range(KV // 2):
@@ -309,16 +306,19 @@
             dv_parts.append(total[8 * i + B : 8 * i + 8])
     obk[...] = jnp.concatenate(dk_parts, axis=1).astype(BF16)
     obv[...] = jnp.concatenate(dv_parts, axis=1).astype(BF16)
-    for i, (a, b) in enumerate([(obk, bk_out), (obv, bv_out)]):
-        oc = pltpu.make_async_copy(a, b, out_sem.at[KV + 3 + i])
-        oc.start()
-        out_copies.append(oc)
     pltpu.make_async_copy(gat.at[pl.ds(1, n - 1)], gat.at[pl.ds(1, n - 1)], ag_send).wait()
     for pair in range(KV // 2):
         left = sbuf.at[pair, pl.ds(1, n - 1)]
         pltpu.make_async_copy(left, left, rs_send.at[pair]).wait()
-    for oc in out_copies:
-        oc.wait()
+
+
+def hand_out(*refs):
+    sem = refs[12]
+    copies = [pltpu.make_async_copy(refs[i], refs[6 + i], sem.at[i]) for i in range(6)]
+    for c in copies:
+        c.start()
+    for c in copies:
+        c.wait()
 
 
 def local(n, *args):
@@ -328,10 +328,12 @@
     out_shape = [jax.ShapeDtypeStruct(x.shape, BF16) for x in (rq, bq, rk, rv, bk, bv)]
     vm = pltpu.VMEM
     any_spec = pl.BlockSpec(memory_space=pl.ANY)
+    hbm_spec = pl.BlockSpec(memory_space=pltpu.HBM)
     vmem_spec = pl.BlockSpec(memory_space=pltpu.VMEM)
     scratch = [
         vm(rq.shape, BF16), vm(rg.shape, BF16), vm(rk.shape, BF16), vm(rv.shape, BF16),
         vm(bq.shape, BF16), vm(bg.shape, BF16), vm(bk.shape, BF16), vm(bv.shape, BF16),
+        vm((1, n), jnp.int32), vm((1, n), jnp.int32), vm((1, n), jnp.int32),
         vm((HEADS * B, D), F32), vm((HEADS * B, D), F32),
         vm((2 * KV * B, D), F32), vm((n, 2 * KV * B, D), BF16),
         vm((KV, rows, D), BF16), vm((KV, rows, D), BF16),
@@ -339,22 +341,29 @@
         vm((SPAN, D), F32), vm((SPAN, D), F32), vm((KV, 8, WIDE), F32),
         vm((KV, keys, WIDE + D), BF16), vm((KV, keys, WIDE + D), BF16),
         vm((KV // 2, n, 16, D), BF16), vm((KV // 2, n, 16, D), BF16),
-        vm(rq.shape, BF16), vm(bq.shape, BF16), vm(rk.shape, BF16), vm(rv.shape, BF16),
-        vm(bk.shape, BF16), vm(bv.shape, BF16),
-        pltpu.SemaphoreType.DMA((6 + 2 * KV,)), pltpu.SemaphoreType.DMA((KV + 5,)),
+        pltpu.SemaphoreType.DMA((9 + 2 * KV,)),
         pltpu.SemaphoreType.DMA, pltpu.SemaphoreType.DMA,
         pltpu.SemaphoreType.DMA((KV // 2,)), pltpu.SemaphoreType.DMA((KV // 2,)),
     ]
-    return pl.pallas_call(
+    ins = [rq, bq, rk, rv, bk, bv, rg, bg] + [x.reshape(1, n) for x in (ss, bc, fs)]
+    made = pl.pallas_call(
         functools.partial(kernel, n),
-        out_shape=out_shape,
-        in_specs=[any_spec] * 8 + [vmem_spec] * 3,
-        out_specs=[any_spec] * 6,
+        out_shape=[pltpu.VMEM(x.shape, BF16) for x in out_shape],
+        in_specs=[hbm_spec] * 11,
+        out_specs=[vmem_spec] * 6,
         scratch_shapes=scratch,
         compiler_params=pltpu.CompilerParams(
-            collective_id=0, has_side_effects=True, vmem_limit_bytes=50 * 2**20
+            collective_id=0, has_side_effects=True, vmem_limit_bytes=VMEM_LIMIT
         ),
-    )(rq, bq, rk, rv, bk, bv, rg, bg, ss.reshape(1, n), bc.reshape(1, n), fs.reshape(1, n))
+    )(*[pltpu.with_memory_space_constraint(x, pltpu.HBM) for x in ins])
+    return pl.pallas_call(
+        hand_out,
+        out_shape=[pltpu.HBM(x.shape, BF16) for x in out_shape],
+        in_specs=[any_spec] * 6,
+        out_specs=[hbm_spec] * 6,
+        scratch_shapes=[pltpu.SemaphoreType.DMA((6,))],
+        compiler_params=pltpu.CompilerParams(vmem_limit_bytes=2**20),
+    )(*made)
 
 
 def solution(mesh):

time: 31.2 us -> 20.3 us (0.65)
  local copies, waits for them, and re-layouts: 11.2 us -> 0 us
  Pallas kernels: 18.9 us -> 19.4 us
    unnamed x28 -> x0, local copies, waits for them, and re-layouts: 11.2 us -> none
    pallas_call x1 -> x2, Pallas kernels: 18.9 us -> 19.4 us  [the longest x1 18.3 us: local(): pl.pallas_call(functools.partial(kernel, n), out_shape=[pltpu.VMEM(x.shap...]
where the time goes in v2:
time: 20.3 us; the launch traced here: 20 us
  Pallas kernels  19.4 us (96%)
  between operations  0.64 us (3%)
    pallas_call x1, Pallas kernels, local(): pl.pallas_call(functools.partial(kernel, n), out_shape=[pltpu.VMEM(x.shap...  18.3 us
    pallas_call x1, Pallas kernels, local(): pl.pallas_call(hand_out, out_shape=[pltpu.HBM(x.shape, BF16) for x in out...  1.11 us

profile of v2, /device:TPU:0, one launch (start us, length us, event | category | flops | bytes accessed | tf_op | source)
XLA Modules:
  0.0 20.0 jit_solution(3808934867545628943)
XLA Ops:
  0.6 18.3 %shard_map.154 = (bf16[128,4096]{1,0:T(8,128)(2,1)S(1)}, bf16[4,4096]{1,0:T(4,128)(2,1)S(1)}, bf16[128,512]{1,0:T(8,128)(2,1)S(1)}, bf16[128,512]{1,0:T(8,128)(2...) custom-call(bf16[128,4096]{1,0:T(8,128)(2,1)} %rq.1, bf16[4,4096]{1,0:T(4,128)(2,1)} %bq.1, ...), custom_call_target="tpu_custom_call" | custom-call | tf_op jit(solution)/shard_map/pallas_call | solution.py:349
  18.9 1.1 %shard_map.155 = (bf16[128,4096]{1,0:T(8,128)(2,1)}, bf16[4,4096]{1,0:T(4,128)(2,1)}, bf16[128,512]{1,0:T(8,128)(2,1)}, bf16[128,512]{1,0:T(8,128)(2,1)}, bf16[4...) custom-call(bf16[128,4096]{1,0:T(8,128)(2,1)S(1)} %get-tuple-element.12.refs_0_, bf16[4,4096]{1,0:T(4,128)(2,1)S(1)} %get-tuple-element.13.refs_1_, ...), custom_call_target="tpu_custom_call" | custom-call | tf_op jit(solution)/shard_map/pallas_call | solution.py:359

commit v3 on v2

--- a/solution.py
+++ b/solution.py
@@ -62,11 +62,14 @@
     me = lax.axis_index("seq")
     rows = n * B
 
+    def ahead(d):
+        return jnp.where(me + d >= n, me + d - n, me + d)
+
     barrier = pltpu.get_barrier_semaphore()
 
     def greet(d):
         pl.semaphore_signal(
-            barrier, inc=1, device_id={"seq": lax.rem(me + d, n)}, device_id_type=MESH
+            barrier, inc=1, device_id={"seq": ahead(d)}, device_id_type=MESH
         )
 
     each(n, greet)
@@ -79,29 +82,6 @@
     small[0].start()
     small[1].start()
 
-    small[0].wait()
-    small[1].wait()
-    bk32 = bks[...].astype(F32)
-    bv32 = bvs[...].astype(F32)
-    for kv in range(KV):
-        msg[kv * B : (kv + 1) * B, :] = bk32[:, kv * D : (kv + 1) * D]
-        msg[(KV + kv) * B : (KV + kv + 1) * B, :] = bv32[:, kv * D : (kv + 1) * D]
-    gat[0] = msg[...].astype(BF16)
-
-    pl.semaphore_wait(barrier, n - 1)
-
-    def gather_copy(d):
-        return pltpu.make_async_remote_copy(
-            src_ref=gat.at[0],
-            dst_ref=gat.at[d],
-            send_sem=ag_send,
-            recv_sem=ag_recv,
-            device_id={"seq": lax.rem(me + d, n)},
-            device_id_type=MESH,
-        )
-
-    each(n, lambda d: gather_copy(d).start())
-
     for c in small[2:]:
         c.start()
     large = []
@@ -113,6 +93,30 @@
         cq.start()
         cg.start()
         large.append((cq, cg))
+
+    small[0].wait()
+    small[1].wait()
+    bk32 = bks[...].astype(F32)
+    bv32 = bvs[...].astype(F32)
+    for kv in range(KV):
+        msg[kv * B : (kv + 1) * B, :] = bk32[:, kv * D : (kv + 1) * D]
+        msg[(KV + kv) * B : (KV + kv + 1) * B, :] = bv32[:, kv * D : (kv + 1) * D]
+    gat[0] = msg[...].astype(BF16)
+
+    pl.semaphore_wait(barrier, n - 1)
+
+    def gather_copy(d):
+        return pltpu.make_async_remote_copy(
+            src_ref=gat.at[0],
+            dst_ref=gat.at[d],
+            send_sem=ag_send,
+            recv_sem=ag_recv,
+            device_id={"seq": ahead(d)},
+            device_id_type=MESH,
+        )
+
+    each(n, lambda d: gather_copy(d).start())
+
     for c in small[2:]:
         c.wait()
 
@@ -314,7 +318,12 @@
 
 def hand_out(*refs):
     sem = refs[12]
-    copies = [pltpu.make_async_copy(refs[i], refs[6 + i], sem.at[i]) for i in range(6)]
+    copies = [pltpu.make_async_copy(refs[i], refs[6 + i], sem.at[i]) for i in range(1, 6)]
+    for i in range(4):
+        part = pl.ds(i * SPAN // 4, SPAN // 4)
+        copies.append(
+            pltpu.make_async_copy(refs[0].at[part], refs[6].at[part], sem.at[(0, 6, 7, 8)[i]])
+        )
     for c in copies:
         c.start()
     for c in copies:
@@ -361,7 +370,7 @@
         out_shape=[pltpu.HBM(x.shape, BF16) for x in out_shape],
         in_specs=[any_spec] * 6,
         out_specs=[hbm_spec] * 6,
-        scratch_shapes=[pltpu.SemaphoreType.DMA((6,))],
+        scratch_shapes=[pltpu.SemaphoreType.DMA((9,))],
         compiler_params=pltpu.CompilerParams(vmem_limit_bytes=2**20),
     )(*made)
 

time: 20.3 us -> 20.3 us (level)
  no operation moved by 1% of the time
where the time goes in v3:
time: 20.3 us; the launch traced here: 20.1 us
  Pallas kernels  19.4 us (96%)
  between operations  0.64 us (3%)
    pallas_call x1, Pallas kernels, local(): pl.pallas_call(functools.partial(kernel, n), out_shape=[pltpu.VMEM(x.shap...  18.3 us
    pallas_call x1, Pallas kernels, local(): pl.pallas_call(hand_out, out_shape=[pltpu.HBM(x.shape, BF16) for x in out...  1.15 us

profile of v3, /device:TPU:0, one launch (start us, length us, event | category | flops | bytes accessed | tf_op | source)
XLA Modules:
  0.0 20.1 jit_solution(4927782734729900811)
XLA Ops:
  0.6 18.3 %shard_map.154 = (bf16[128,4096]{1,0:T(8,128)(2,1)S(1)}, bf16[4,4096]{1,0:T(4,128)(2,1)S(1)}, bf16[128,512]{1,0:T(8,128)(2,1)S(1)}, bf16[128,512]{1,0:T(8,128)(2...) custom-call(bf16[128,4096]{1,0:T(8,128)(2,1)} %rq.1, bf16[4,4096]{1,0:T(4,128)(2,1)} %bq.1, ...), custom_call_target="tpu_custom_call" | custom-call | tf_op jit(solution)/shard_map/pallas_call | solution.py:358
  18.9 1.1 %shard_map.155 = (bf16[128,4096]{1,0:T(8,128)(2,1)}, bf16[4,4096]{1,0:T(4,128)(2,1)}, bf16[128,512]{1,0:T(8,128)(2,1)}, bf16[128,512]{1,0:T(8,128)(2,1)}, bf16[4...) custom-call(bf16[128,4096]{1,0:T(8,128)(2,1)S(1)} %get-tuple-element.12.refs_0_, bf16[4,4096]{1,0:T(4,128)(2,1)S(1)} %get-tuple-element.13.refs_1_, ...), custom_call_target="tpu_custom_call" | custom-call | tf_op jit(solution)/shard_map/pallas_call | solution.py:368
